TPU v7x, 32 devices: a whole 2x2x4 slice. The times are simulated.
32 devices in a mesh: groups: 2 (over x), slide: 16 (over z, y, core).
Axes of the slice: x: 2, y: 2, z: 4, core: 2. Of those that a mesh axis runs over, the one named last changes fastest.
Arguments:
- tile_tokens: bfloat16 [24576, 1536], P(('groups', 'slide')), parts along dimension 0, may hold values from -6 to 6
- tile_counts: int32 [32], P('groups'), parts along dimension 0, may hold values from 1 to 3, 24 in all
- w_gate_up: bfloat16 [1536, 4096], replicated, may hold values from -0.15625 to 0.15625
- w_down: bfloat16 [2048, 1536], replicated, may hold values from -0.125 to 0.125
- w_tile_proj: bfloat16 [1536, 768], P('slide'), may hold values from -0.15625 to 0.15625
- slide_rows: bfloat16 [24576, 768], P(('groups', 'slide')), parts along dimension 0, may hold values from -6 to 6
- w_qkv: bfloat16 [768, 2304], P('slide'), may hold values from -5 to 5
- w_out: bfloat16 [768, 768], P('slide'), may hold values from -0.875 to 0.875
Outputs:
- slide_out: bfloat16 [24576, 768], P(('groups', 'slide')), parts along dimension 0
- tile_embeddings: bfloat16 [96, 1536], P(('groups', 'slide')), parts along dimension 0
There are 2 independent parts, one for each index of `groups`. A program takes and returns all parts, laid end to end along the dimension named above; an argument that names none is the same for every part. Nothing has to cross between parts.
Inputs may be any that keep to these rules, and one draw needn't show every extreme that they name: `tile_counts`: each device's number of tiles; over the devices they sum to 24.
All inputs are finite; a program needn't handle non-finite values.
Results may differ from a plain program's by a relative error of at most 0.007.
The roundings to bfloat16 on the way count: a program that leaves them out, or rounds other values in their place, can miss the bound.
Values may be sent and summed in bfloat16 or wider, within the bound.
A program may use at most 192 MiB of HBM per device.

v0:
```python
import functools
import math

import jax
import jax.numpy as jnp
import numpy as np
from jax import lax
from jax.experimental import pallas as pl
from jax.experimental.pallas import tpu as pltpu
from jax.sharding import PartitionSpec as P

TT = 256
TMAX = 3
HEADS = 16
HD = 48
DILATION = 4
LANES = 128

tile_epsilon = 1e-06
slide_epsilon = 1e-05
SCALE = HD ** (-0.5) * math.log2(math.e)
BLOCK_OF = {0: 0, 2: 1, 1: 2, 3: 3}

f32 = jnp.float32
bf16 = jnp.bfloat16
VMEM = pl.BlockSpec(memory_space=pltpu.VMEM)
SMEM = pl.BlockSpec(memory_space=pltpu.SMEM)
PARAMS = pltpu.CompilerParams(vmem_limit_bytes=56 * 1024 * 1024)


def normalize(matrix, epsilon):
    average = jnp.mean(matrix, axis=-1, keepdims=True)
    centered = matrix - average
    variance = jnp.mean(centered * centered, axis=-1, keepdims=True)
    return centered * lax.rsqrt(variance + epsilon)


def dot(a, b):
    return jnp.dot(a, b, preferred_element_type=f32)


def dot_nt(a, b):
    return lax.dot_general(a, b, (((1,), (1,)), ((), ())), preferred_element_type=f32)


def split3(value):
    high = value.astype(bf16)
    rest = value - high.astype(f32)
    middle = rest.astype(bf16)
    return high, middle, (rest - middle.astype(f32)).astype(bf16)


def window(head):
    first = head * HD
    start = first // LANES * LANES
    width = LANES if first + HD <= start + LANES else 2 * LANES
    return start, width, first - start


def lane_mask(width, offset):
    lane = lax.broadcasted_iota(jnp.int32, (1, width), 1)
    return (lane >= offset) & (lane < offset + HD)


def permutation(rows, transposed):
    each = rows // DILATION
    stored = lax.broadcasted_iota(jnp.int32, (rows, rows), 1 if transposed else 0)
    position = lax.broadcasted_iota(jnp.int32, (rows, rows), 0 if transposed else 1)
    block = sum((stored >= each * i).astype(jnp.int32) for i in range(1, DILATION))
    phase = jnp.where(block == 1, 2, jnp.where(block == 2, 1, block))
    wanted = (stored - block * each) * DILATION + phase
    return jnp.where(position == wanted, 1.0, 0.0).astype(bf16)


def tile_kernel(count_ref, tokens_ref, gate_ref, up_ref, down_ref, out_ref, normed, mixed):
    step = pl.program_id(0)

    @pl.when(step == 0)
    def _():
        mixed[...] = jnp.zeros_like(mixed)
        for slot in range(TMAX):
            rows = pl.ds(slot * TT, TT)
            tokens = tokens_ref[rows, :].astype(f32)
            normed[rows, :] = normalize(tokens, tile_epsilon).astype(bf16)
            mixed[slot : slot + 1, :] = jnp.sum(tokens, axis=0, keepdims=True)

    for slot in range(TMAX):

        @pl.when(slot < count_ref[0])
        def _():
            rows = normed[pl.ds(slot * TT, TT), :]
            gate = dot(rows, gate_ref[...])
            up = dot(rows, up_ref[...])
            hidden = (gate * jax.nn.sigmoid(gate) * up).astype(bf16).astype(f32)
            total = jnp.broadcast_to(jnp.sum(hidden, axis=0, keepdims=True), (8, hidden.shape[1]))
            parts = split3(total)
            down = down_ref[...]
            add = dot(parts[0], down) + dot(parts[1], down) + dot(parts[2], down)
            mixed[slot : slot + 1, :] += add[:1]

    @pl.when(step == pl.num_programs(0) - 1)
    def _():
        out_ref[...] = normalize(mixed[...] / TT, tile_epsilon).astype(bf16)


def encode_tiles(my_count, tile_tokens, w_gate_up, w_down):
    rows, width = tile_tokens.shape
    hidden = w_down.shape[0]
    block = 512
    steps = hidden // block
    return pl.pallas_call(
        tile_kernel,
        grid=(steps,),
        out_shape=jax.ShapeDtypeStruct((16, width), bf16),
        in_specs=[
            SMEM,
            pl.BlockSpec((rows, width), lambda i: (0, 0)),
            pl.BlockSpec((width, block), lambda i: (0, i)),
            pl.BlockSpec((width, block), lambda i: (0, i + steps)),
            pl.BlockSpec((block, width), lambda i: (i, 0)),
        ],
        out_specs=pl.BlockSpec((16, width), lambda i: (0, 0)),
        scratch_shapes=[pltpu.VMEM((rows, width), bf16), pltpu.VMEM((16, width), f32)],
        compiler_params=PARAMS,
        cost_estimate=pl.CostEstimate(
            flops=2 * rows * width * 2 * hidden, bytes_accessed=22 * 1024 * 1024, transcendentals=0
        ),
        name="tile_block",
    )(my_count, tile_tokens, w_gate_up, w_gate_up, w_down)


def project_kernel(
    repeat, count_ref, emb_ref, proj_ref, rows_ref, qkv_ref, now_ref, q_ref, k_ref, v_ref, far_ref, send_ref
):
    rows, width = rows_ref.shape
    each, half = rows // DILATION, rows // 2
    fresh = dot(emb_ref[...], proj_ref[...]).astype(bf16).astype(f32)
    keep = lax.broadcasted_iota(jnp.int32, (16, 1), 0) < count_ref[0]
    now_ref[...] = rows_ref[...]
    now_ref[0:16, :] = jnp.where(keep, fresh, rows_ref[0:16, :].astype(f32)).astype(bf16)
    normed = normalize(now_ref[...].astype(f32), slide_epsilon).astype(bf16)
    normed = dot(permutation(rows, False), normed).astype(bf16)
    for index, ref in enumerate((q_ref, k_ref, v_ref)):
        ref[...] = dot(normed, qkv_ref[:, index * width : (index + 1) * width]).astype(bf16)
    lane = lax.broadcasted_iota(jnp.int32, (1, width), 1)
    head = sum((lane >= HD * i).astype(jnp.int32) for i in range(1, HEADS))
    even = (head & 1) == 0
    for index, ref in enumerate((k_ref, v_ref)):
        far_ref[index * half : (index + 1) * half, :] = jnp.where(
            even, ref[0:half, :].astype(f32), ref[half:rows, :].astype(f32)
        ).astype(bf16)
    tail_rows = each // 8
    for h in range(HEADS):
        first = BLOCK_OF[h % DILATION] * each
        pieces = [
            ref[first : first + each, h * HD : (h + 1) * HD].astype(f32)
            for ref in (q_ref, k_ref, v_ref)
        ]
        main = jnp.concatenate([pieces[0], pieces[1], pieces[2][:, :32]], axis=1)
        tail = jnp.concatenate(
            [pieces[2][r * tail_rows : (r + 1) * tail_rows, 32:] for r in range(8)], axis=1
        )
        whole = jnp.concatenate([main, tail], axis=0).astype(bf16)
        for again in range(repeat):
            send_ref[h * repeat + again] = whole


def project(repeat, my_count, embedded, proj_full, slide_rows, qkv_full):
    rows, width = slide_rows.shape
    each = rows // DILATION
    square = jax.ShapeDtypeStruct((rows, width), bf16)
    return pl.pallas_call(
        functools.partial(project_kernel, repeat),
        out_shape=[square] * 5
        + [jax.ShapeDtypeStruct((HEADS * repeat, each + each // 8, LANES), bf16)],
        in_specs=[SMEM] + [VMEM] * 4,
        out_specs=[VMEM] * 6,
        compiler_params=PARAMS,
        cost_estimate=pl.CostEstimate(
            flops=2 * rows * width * 4 * width, bytes_accessed=16 * 1024 * 1024, transcendentals=0
        ),
        name="project",
    )(my_count, embedded, proj_full, slide_rows, qkv_full)


def near_kernel(q_ref, k_ref, v_ref, far_ref, out_ref, lse_ref):
    rows = q_ref.shape[0]
    half = rows // 2
    chunk = 128
    for h in range(8):
        start, width, offset = window(h)
        lanes = slice(start, start + width)
        mask = lane_mask(width, offset)
        outside = 0 if offset > 0 else HD
        parity = h % 2
        same = slice(parity * half, parity * half + half)
        other = slice((1 - parity) * half, (1 - parity) * half + half)

        def ones_outside(value):
            return jnp.where(mask, value.astype(f32), 1.0).astype(bf16)

        keys_same, keys_other, keys_far = k_ref[same, lanes], k_ref[other, lanes], far_ref[:half, lanes]
        values_same = ones_outside(v_ref[same, lanes])
        values_other = ones_outside(v_ref[other, lanes])
        values_far = ones_outside(far_ref[half:, lanes])
        for part in range(rows // chunk):
            at = slice(part * chunk, (part + 1) * chunk)
            in_pair = same.start <= at.start < same.stop
            queries = jnp.where(mask, q_ref[at, lanes].astype(f32), 0.0).astype(bf16)
            scores = [dot_nt(queries, keys_same), dot_nt(queries, keys_other)]
            values = [values_same, values_other]
            if in_pair:
                scores.append(dot_nt(queries, keys_far))
                values.append(values_far)
            peaks = [jnp.max(s, axis=1, keepdims=True) for s in scores]
            peak = functools.reduce(jnp.maximum, peaks) * SCALE
            total = 0.0
            for index, (s, v) in enumerate(zip(scores, values)):
                shift = peak - 1.0 if in_pair and index == 0 else peak
                total = total + dot(jnp.exp2(s * SCALE - shift).astype(bf16), v)
            mass = total[:, outside : outside + 1]
            out_ref[at, lanes] = jnp.where(mask, total * (1.0 / mass), out_ref[at, lanes])
            lse_ref[at, lanes] = jnp.where(mask, peak + jnp.log2(mass), lse_ref[at, lanes])


def attend_near(queries, key_rows, value_rows, far):
    rows, width = queries.shape
    spec = pl.BlockSpec((rows, 8 * HD), lambda i: (0, i))
    return pl.pallas_call(
        near_kernel,
        grid=(width // (8 * HD),),
        out_shape=[jax.ShapeDtypeStruct((rows, width), f32)] * 2,
        in_specs=[spec] * 4,
        out_specs=[spec] * 2,
        compiler_params=PARAMS,
        cost_estimate=pl.CostEstimate(
            flops=12 * 10**9, bytes_accessed=10 * 1024 * 1024, transcendentals=12 * 10**6
        ),
        name="near_attention",
    )(queries, key_rows, value_rows, far)


def wide_kernel(repeat, part_ref, recv_ref, out_ref, keys, values):
    count, packed, _ = recv_ref.shape
    each = packed * 8 // 9
    tail_rows = each // 8
    lane = lax.broadcasted_iota(jnp.int32, (1, LANES), 1)
    step = pl.program_id(0)

    @pl.when(step == 0)
    def _():
        @pl.loop(0, count)
        def _(source):
            block = recv_ref[source]
            at = pl.ds(pl.multiple_of(source * each, each), each)
            keys[at, :] = block[:each]
            wide = block.astype(f32)
            tail = wide[each:]
            tails = [tail] + [pltpu.roll(tail, LANES - 16 * r, axis=1) for r in range(1, 8)]
            tail = jnp.concatenate(tails, axis=0)
            picked = jnp.where(lane >= 96, wide[:each], jnp.where(lane < 16, tail, 1.0))
            values[at, :] = picked.astype(bf16)

    queries = pltpu.roll(recv_ref[step * repeat + part_ref[0]].astype(f32)[:each], HD, axis=1)
    queries = jnp.where((lane >= HD) & (lane < 2 * HD), queries, 0.0).astype(bf16)
    scores = dot_nt(queries, keys[...])
    peak = jnp.max(scores, axis=1, keepdims=True) * SCALE
    total = dot(jnp.exp2(scores * SCALE - peak).astype(bf16), values[...])
    total = pltpu.roll(total, 32, axis=1)
    mass = total[:, HD : HD + 1]
    lse = peak + jnp.log2(mass)
    high, middle, low = [piece.astype(f32) for piece in split3(lse)]
    out = jnp.where(
        lane < HD,
        total * (1.0 / mass),
        jnp.where(lane == HD, high, jnp.where(lane == HD + 1, middle, low)),
    )
    upper = pltpu.roll(out[each // 2 :], 64, axis=1)
    out_ref[0] = jnp.where(lane < 64, out[: each // 2], upper).astype(bf16)


def attend_wide(repeat, part, received):
    count, packed, _ = received.shape
    each = packed * 8 // 9
    steps = count // repeat
    return pl.pallas_call(
        functools.partial(wide_kernel, repeat),
        grid=(steps,),
        out_shape=jax.ShapeDtypeStruct((steps, each // 2, LANES), bf16),
        in_specs=[SMEM, pl.BlockSpec(received.shape, lambda i: (0, 0, 0))],
        out_specs=pl.BlockSpec((1, each // 2, LANES), lambda i: (i, 0, 0)),
        scratch_shapes=[pltpu.VMEM((count * each, LANES), bf16)] * 2,
        compiler_params=PARAMS,
        cost_estimate=pl.CostEstimate(
            flops=10 * 10**9, bytes_accessed=2 * 1024 * 1024, transcendentals=10**7
        ),
        name="wide_attention",
    )(part, received)


def finish_kernel(near_ref, lse_ref, wide_ref, out_w_ref, now_ref, out_ref, mixed):
    rows, width = near_ref.shape
    each = rows // DILATION
    mixed[...] = near_ref[...]
    for h in range(HEADS):
        start, span, offset = window(h)
        lanes = slice(start, start + span)
        mask = lane_mask(span, offset)
        first = BLOCK_OF[h % DILATION] * each
        at = slice(first, first + each)
        block = wide_ref[h].astype(f32)
        block = jnp.concatenate([block, pltpu.roll(block, 64, axis=1)], axis=0)
        far_lse = block[:, HD : HD + 1] + block[:, HD + 1 : HD + 2] + block[:, HD + 2 : HD + 3]
        if span > LANES:
            block = jnp.concatenate([block, jnp.zeros_like(block)], axis=1)
        far_out = pltpu.roll(block, offset, axis=1) if offset else block
        near_lse = jnp.where(mask, lse_ref[at, lanes], 0.0)
        highest = jnp.maximum(near_lse, far_lse)
        near_weight, far_weight = jnp.exp2(near_lse - highest), jnp.exp2(far_lse - highest)
        merged = (near_weight * near_ref[at, lanes] + far_weight * far_out) / (near_weight + far_weight)
        mixed[at, lanes] = jnp.where(mask, merged, mixed[at, lanes])
    attended = dot(permutation(rows, True), mixed[...].astype(bf16)).astype(bf16)
    out_ref[...] = (now_ref[...].astype(f32) + dot(attended, out_w_ref[...])).astype(bf16)


def finish(near_out, near_lse, wide, out_full, slide_now):
    rows, width = slide_now.shape
    return pl.pallas_call(
        finish_kernel,
        out_shape=jax.ShapeDtypeStruct((rows, width), bf16),
        in_specs=[VMEM] * 5,
        out_specs=VMEM,
        scratch_shapes=[pltpu.VMEM((rows, width), f32)],
        compiler_params=PARAMS,
        cost_estimate=pl.CostEstimate(
            flops=4 * rows * width * width, bytes_accessed=9 * 1024 * 1024, transcendentals=0
        ),
        name="finish",
    )(near_out, near_lse, wide, out_full, slide_now)


def body(tile_tokens, tile_counts, w_gate_up, w_down, w_tile_proj, slide_rows, w_qkv, w_out):
    size = lax.axis_size("slide")
    repeat = size // HEADS
    me = lax.axis_index("slide")
    my_count = lax.dynamic_slice(tile_counts, (me,), (1,))
    qkv_full = lax.all_gather(w_qkv, "slide", axis=0, tiled=True)
    proj_full = lax.all_gather(w_tile_proj, "slide", axis=0, tiled=True)
    out_full = lax.all_gather(w_out, "slide", axis=0, tiled=True)
    embedded = encode_tiles(my_count, tile_tokens, w_gate_up, w_down)
    keep = jnp.arange(TMAX, dtype=jnp.int32)[:, None] < my_count
    tile_embeddings = jnp.where(keep, embedded[:TMAX], jnp.zeros((), bf16))
    slide_now, queries, key_rows, value_rows, far, send = project(
        repeat, my_count, embedded, proj_full, slide_rows, qkv_full
    )
    far = lax.ppermute(far, "slide", [(source, source ^ 1) for source in range(size)])
    received = lax.all_to_all(send, "slide", 0, 0, tiled=True)
    near_out, near_lse = attend_near(queries, key_rows, value_rows, far)
    wide = attend_wide(repeat, (me % repeat).astype(jnp.int32)[None], received)
    wide = jnp.repeat(wide, repeat, axis=0) if repeat > 1 else wide
    wide = lax.all_to_all(wide, "slide", 0, 0, tiled=True)
    if repeat > 1:
        wide = lax.dynamic_index_in_dim(
            wide.reshape(HEADS, repeat, *wide.shape[1:]), me % repeat, 1, keepdims=False
        )
    return finish(near_out, near_lse, wide, out_full, slide_now), tile_embeddings


def solution(mesh):
    return jax.shard_map(
        body,
        mesh=mesh,
        in_specs=(
            P(("groups", "slide"), None),
            P("groups"),
            P(),
            P(),
            P("slide", None),
            P(("groups", "slide"), None),
            P("slide", None),
            P("slide", None),
        ),
        out_specs=(P(("groups", "slide"), None), P(("groups", "slide"), None)),
        check_vma=False,
    )
```

profile of v0, /device:TPU:0, one launch (start us, length us, event | category | flops | bytes accessed | tf_op | source)
XLA Modules:
  0.0 227.3 jit_solution(6375530641965666256)
XLA Ops:
  7.2 0.0 all-gather.4.cloned.1.call-start
  7.2 0.7 all-gather.4.cloned.1.call-update
  7.9 0.0 all-gather.6.cloned.1.call-start
  7.9 0.7 all-gather.6.cloned.1.call-update
  8.7 1.2 dynamic_slice.3.count_ref
  9.9 14.2 %tile_block.1.emb_ref = bf16[16,1536]{1,0:T(8,128)(2,1)} custom-call(s32[1]{0:T(128)} %dynamic_slice.3.count_ref, bf16[768,1536]{1,0:T(8,128)(2,1)} %tokens_ref.1, bf16[1536,4096]{1,0:T(8,128)(2,1)} %up_ref.1, bf16[1536,4096]{1,0:T(8,128)(2,1)} %up_ref.1, bf16[2048,1536]{1,0:T(8,128)(2,1)} %down_ref.1), custom_call_target="tpu_custom_call" | custom-call | flops 9663676416 | bytes 23068672 | tf_op jit(solution)/shard_map/tile_block/pallas_call | solution.py:111
  24.0 31.3 %all-gather.4.cloned.1.call-done.proj_ref = bf16[1536,768]{1,0:T(8,128)(2,1)} async-done(((bf16[96,768]{1,0:T(8,128)(2,1)}), bf16[1536,768]{1,0:T(8,128)(2,1)}) %all-gather.4.cloned.1.call-update) | async-done | bytes 2359312 | tf_op jit(solution)/shard_map/all_gather | solution.py:348
  55.3 48.3 %all-gather.6.cloned.1.call-done.qkv_ref = bf16[768,2304]{1,0:T(8,128)(2,1)} async-done(((bf16[48,2304]{1,0:T(8,128)(2,1)}), bf16[768,2304]{1,0:T(8,128)(2,1)}) %all-gather.6.cloned.1.call-update) | async-done | bytes 3538960 | tf_op jit(solution)/shard_map/all_gather | solution.py:347
  103.6 11.3 %project.1 = (bf16[768,768]{1,0:T(8,128)(2,1)}, bf16[768,768]{1,0:T(8,128)(2,1)}, bf16[768,768]{1,0:T(8,128)(2,1)}, bf16[768,768]{1,0:T(8,128)(2,1)}, bf16[768,7...) custom-call(s32[1]{0:T(128)} %dynamic_slice.3.count_ref, bf16[16,1536]{1,0:T(8,128)(2,1)} %tile_block.1.emb_ref, ...), custom_call_target="tpu_custom_call" | custom-call | flops 3623878656 | bytes 16777216 | tf_op jit(solution)/shard_map/project/pallas_call | solution.py:172
  115.0 0.0 copy-start.2
  115.0 3.8 %all-to-all-start = ((bf16[16,216,128]{2,1,0:T(8,128)(2,1)}), bf16[16,216,128]{2,1,0:T(8,128)(2,1)S(1)}, u32[]{:S(2)}, u32[]{:S(2)}) async-start(bf16[16,216,128]{2,1,0:T(8,128)(2,1)} %get-tuple-element.16), calls=%async_computation | async-start | bytes 1769472 | tf_op jit(solution)/shard_map/all_to_all | solution.py:357
  118.8 0.0 all-gather.8.cloned.1.call-start
  118.9 0.7 all-gather.8.cloned.1.call-update
  119.6 0.7 iota_compare_fusion
  120.2 0.0 copy-done.2
  120.2 0.5 collective-permute-start
  120.7 1.4 slice_select_fusion
  122.1 17.8 %all-to-all-done.recv_ref = bf16[16,216,128]{2,1,0:T(8,128)(2,1)S(1)} async-done(((bf16[16,216,128]{2,1,0:T(8,128)(2,1)}), bf16[16,216,128]{2,1,0:T(8,128)(2,1)S(1)}, u32[]{:S(2)}, u32[]{:S(2)}) %all-to-all-start) | async-done | bytes 884768 | tf_op jit(solution)/shard_map/all_to_all | solution.py:357
  139.9 0.0 copy-start.1
  139.9 0.9 copy-done.1
  140.8 24.3 %wide_attention.1 = bf16[16,96,128]{2,1,0:T(8,128)(2,1)} custom-call(s32[1]{0:T(128)} %constant.21.clone.1.part_ref, bf16[16,216,128]{2,1,0:T(8,128)(2,1)} %copy-done.1), custom_call_target="tpu_custom_call" | custom-call | flops 10000000000 | bytes 2097152 | tf_op jit(solution)/shard_map/wide_attention/pallas_call | solution.py:286
  165.1 7.2 %all-to-all-start.1 = ((bf16[16,96,128]{2,1,0:T(8,128)(2,1)}), bf16[16,96,128]{2,1,0:T(8,128)(2,1)S(1)}, u32[]{:S(2)}, u32[]{:S(2)}) async-start(bf16[16,96,128]{2,1,0:T(8,128)(2,1)} %wide_attention.1), calls=%async_computation.1 | async-start | bytes 786432 | tf_op jit(solution)/shard_map/all_to_all | solution.py:361
  172.3 0.0 collective-permute-done.far_ref
  172.4 0.0 copy-start.3
  172.4 1.0 copy-done.3
  173.4 39.3 %near_attention.1 = (f32[768,768]{1,0:T(8,128)}, f32[768,768]{1,0:T(8,128)}) custom-call(bf16[768,768]{1,0:T(8,128)(2,1)} %get-tuple-element.10.q_ref, bf16[768,768]{1,0:T(8,128)(2,1)} %get-tuple-element.11.k_ref, bf16[768,768]{1,0:T(8,128)(2,1)} %get-tuple-element.12.v_ref, bf16[768,768]{1,0:T(8,128)(2,1)} %copy-done.3), custom_call_target="tpu_custom_call" | custom-call | flops 12000000000 | bytes 10485760 | tf_op jit(solution)/shard_map/near_attention/pallas_call | solution.py:229
  212.7 0.0 all-gather.8.cloned.1.call-done.out_w_ref
  212.7 0.0 all-to-all-done.1.wide_ref
  212.7 0.0 copy-start
  212.7 0.7 copy-done
  213.5 7.3 %finish.1 = bf16[768,768]{1,0:T(8,128)(2,1)} custom-call(f32[768,768]{1,0:T(8,128)} %get-tuple-element.14.near_ref, f32[768,768]{1,0:T(8,128)} %get-tuple-element.15.lse_ref, bf16[16,96,128]{2,1,0:T(8,128)(2,1)} %copy-done, bf16[768,768]{1,0:T(8,128)(2,1)} %all-gather.8.cloned.1.call-done.out_w_ref, bf16[768,768]{1,0:T(8,128)(2,1)} %get-tuple-element.17.now_ref), custom_call_target="tpu_custom_call" | custom-call | flops 1811939328 | bytes 9437184 | tf_op jit(solution)/shard_map/finish/pallas_call | solution.py:328
Async XLA Ops:
  7.2 48.2 %all-gather.4.cloned.1.call-start = ((), (), s32[]{:S(2)}) async-start(), calls=%async_computation.2 | async-start | bytes 2506752 | tf_op jit(solution)/shard_map/all_gather | solution.py:348
  7.9 95.7 %all-gather.6.cloned.1.call-start = ((), (), s32[]{:S(2)}) async-start(), calls=%async_computation.3 | async-start | bytes 3760128 | tf_op jit(solution)/shard_map/all_gather | solution.py:347
  115.0 5.2 %copy-start.2 = (bf16[768,768]{1,0:T(8,128)(2,1)S(1)}, bf16[768,768]{1,0:T(8,128)(2,1)}, u32[]{:S(2)}) copy-start(bf16[768,768]{1,0:T(8,128)(2,1)} %get-tuple-element.13) | copy-start | bytes 3538948
  115.0 24.9 %all-to-all-start = ((bf16[16,216,128]{2,1,0:T(8,128)(2,1)}), bf16[16,216,128]{2,1,0:T(8,128)(2,1)S(1)}, u32[]{:S(2)}, u32[]{:S(2)}) async-start(bf16[16,216,128]{2,1,0:T(8,128)(2,1)} %get-tuple-element.16), calls=%async_computation | async-start | bytes 1769472 | tf_op jit(solution)/shard_map/all_to_all | solution.py:357
  118.8 93.9 %all-gather.8.cloned.1.call-start = ((), (), s32[]{:S(2)}) async-start(), calls=%async_computation.4 | async-start | bytes 1253376 | tf_op jit(solution)/shard_map/all_gather | solution.py:349
  120.2 52.1 %collective-permute-start = (bf16[768,768]{1,0:T(8,128)(2,1)S(1)}, bf16[768,768]{1,0:T(8,128)(2,1)S(1)}, u32[]{:S(2)}, u32[]{:S(2)}) collective-permute-start(bf16[768,768]{1,0:T(8,128)(2,1)S(1)} %copy-done.2), channel_id=1, source_target_pairs={{0,1},{1,0},{2,3},{3,2},{4,5},{5,4},{6,7},{7,6},{8,9},{9,8},{10,11... | collective-permute-start | bytes 3538952 | tf_op jit(solution)/shard_map/ppermute | solution.py:356
  139.9 0.9 copy-start.1
  165.1 47.6 %all-to-all-start.1 = ((bf16[16,96,128]{2,1,0:T(8,128)(2,1)}), bf16[16,96,128]{2,1,0:T(8,128)(2,1)S(1)}, u32[]{:S(2)}, u32[]{:S(2)}) async-start(bf16[16,96,128]{2,1,0:T(8,128)(2,1)} %wide_attention.1), calls=%async_computation.1 | async-start | bytes 786432 | tf_op jit(solution)/shard_map/all_to_all | solution.py:361
  172.4 1.0 copy-start.3
  212.7 0.7 copy-start
Sparse Core Ops, SparseCore 0:
  10.3 45.0 all-gather.3
  57.6 45.9 all-gather.5
  121.9 41.2 all-gather.7
where the time goes:
time: 228 us; the launch traced here: 227 us
  waiting for transfers between devices  99.4 us (44%)
  Pallas kernels  96.5 us (42%)
  between operations  13.8 us (6%)
  starting transfers between devices  11.6 us (5%)
  local copies, waits for them, and re-layouts  3.91 us (2%)
    all_gather x1, waiting for transfers between devices, body(): qkv_full = lax.all_gather(w_qkv, 'slide', axis=0, tiled=True)  48.3 us
    pallas_call x1, Pallas kernels, attend_near(): pl.pallas_call(near_kernel, grid=(width // (8 * HD),), out_shape=[jax.Sha...  39.3 us
    all_gather x1, waiting for transfers between devices, body(): proj_full = lax.all_gather(w_tile_proj, 'slide', axis=0, tiled=True)  31.3 us
    pallas_call x1, Pallas kernels, attend_wide(): pl.pallas_call(functools.partial(wide_kernel, repeat), grid=(steps,), out...  24.3 us
    all_to_all x1, waiting for transfers between devices, body(): received = lax.all_to_all(send, 'slide', 0, 0, tiled=True)  17.8 us
    pallas_call x1, Pallas kernels, encode_tiles(): pl.pallas_call(tile_kernel, grid=(steps,), out_shape=jax.ShapeDtypeStruct...  14.2 us
    pallas_call x1, Pallas kernels, project(): pl.pallas_call(functools.partial(project_kernel, repeat), out_shape=[squa...  11.3 us
    pallas_call x1, Pallas kernels, finish(): pl.pallas_call(finish_kernel, out_shape=jax.ShapeDtypeStruct((rows, width...  7.31 us
  transfers between devices with their start and end apart: 6, of which 3 were waited for; matrix products, arithmetic and copies ran while one was open for 1% of the time, Pallas kernels for 34%

commit v1 on v0

--- a/solution.py
+++ b/solution.py
@@ -134,7 +134,8 @@
 ):
     rows, width = rows_ref.shape
     each, half = rows // DILATION, rows // 2
-    fresh = dot(emb_ref[...], proj_ref[...]).astype(bf16).astype(f32)
+    fresh = dot(emb_ref[0], proj_ref[:, :width]) + dot(emb_ref[1], proj_ref[:, width:])
+    fresh = fresh.astype(bf16).astype(f32)
     keep = lax.broadcasted_iota(jnp.int32, (16, 1), 0) < count_ref[0]
     now_ref[...] = rows_ref[...]
     now_ref[0:16, :] = jnp.where(keep, fresh, rows_ref[0:16, :].astype(f32)).astype(bf16)
@@ -165,82 +166,107 @@
             send_ref[h * repeat + again] = whole
 
 
-def project(repeat, my_count, embedded, proj_full, slide_rows, qkv_full):
+def project(repeat, my_count, embedded, slide_rows, gathered):
     rows, width = slide_rows.shape
     each = rows // DILATION
     square = jax.ShapeDtypeStruct((rows, width), bf16)
+    packed = (HEADS * repeat, each + each // 8, LANES)
     return pl.pallas_call(
         functools.partial(project_kernel, repeat),
-        out_shape=[square] * 5
-        + [jax.ShapeDtypeStruct((HEADS * repeat, each + each // 8, LANES), bf16)],
-        in_specs=[SMEM] + [VMEM] * 4,
-        out_specs=[VMEM] * 6,
+        grid=(1,),
+        out_shape=[square] * 5 + [jax.ShapeDtypeStruct(packed, bf16)],
+        in_specs=[
+            SMEM,
+            pl.BlockSpec(embedded.shape, lambda i: (0, 0, 0)),
+            pl.BlockSpec((width, 2 * width), lambda i: (0, 2)),
+            pl.BlockSpec((rows, width), lambda i: (0, 0)),
+            pl.BlockSpec((width, 3 * width), lambda i: (0, 0)),
+        ],
+        out_specs=[pl.BlockSpec((rows, width), lambda i: (0, 0))] * 5
+        + [pl.BlockSpec(packed, lambda i: (0, 0, 0))],
         compiler_params=PARAMS,
         cost_estimate=pl.CostEstimate(
             flops=2 * rows * width * 4 * width, bytes_accessed=16 * 1024 * 1024, transcendentals=0
         ),
         name="project",
-    )(my_count, embedded, proj_full, slide_rows, qkv_full)
-
-
-def near_kernel(q_ref, k_ref, v_ref, far_ref, out_ref, lse_ref):
+    )(my_count, embedded, gathered, slide_rows, gathered)
+
+
+def near_kernel(q_ref, k_ref, v_ref, far_ref, out_ref, lse_ref, turned, turned_far):
     rows = q_ref.shape[0]
     half = rows // 2
     chunk = 128
+    turned[...] = k_ref[...].T
+    turned_far[...] = far_ref[:half, :].T
+
+    def score(h, at, in_pair):
+        start, width, offset = window(h)
+        lanes = slice(start, start + width)
+        queries = jnp.where(lane_mask(width, offset), q_ref[at, lanes].astype(f32), 0.0).astype(bf16)
+        scores = [dot(queries, turned[lanes, :])]
+        if in_pair:
+            scores.append(dot(queries, turned_far[lanes, :]))
+        return scores
+
+    def settle(h, at, in_pair, scores, values):
+        start, width, offset = window(h)
+        lanes = slice(start, start + width)
+        mask = lane_mask(width, offset)
+        outside = 0 if offset > 0 else HD
+        peaks = [jnp.max(s, axis=1, keepdims=True) for s in scores]
+        peak = functools.reduce(jnp.maximum, peaks) * SCALE
+        first = h % 2 * half
+        if in_pair:
+            column = lax.broadcasted_iota(jnp.int32, (1, rows), 1)
+            twice = jnp.where((column >= first) & (column < first + half), 1.0, 0.0)
+            weights = jnp.exp2(scores[0] * SCALE - (peak - twice))
+        else:
+            weights = jnp.exp2(scores[0] * SCALE - peak)
+        total = dot(weights.astype(bf16), values[0])
+        if in_pair:
+            total = total + dot(jnp.exp2(scores[1] * SCALE - peak).astype(bf16), values[1])
+        mass = total[:, outside : outside + 1]
+        out_ref[at, lanes] = jnp.where(mask, total * (1.0 / mass), out_ref[at, lanes])
+        lse_ref[at, lanes] = jnp.where(mask, peak + jnp.log2(mass), lse_ref[at, lanes])
+
+    waiting = None
     for h in range(8):
         start, width, offset = window(h)
         lanes = slice(start, start + width)
         mask = lane_mask(width, offset)
-        outside = 0 if offset > 0 else HD
-        parity = h % 2
-        same = slice(parity * half, parity * half + half)
-        other = slice((1 - parity) * half, (1 - parity) * half + half)
-
-        def ones_outside(value):
-            return jnp.where(mask, value.astype(f32), 1.0).astype(bf16)
-
-        keys_same, keys_other, keys_far = k_ref[same, lanes], k_ref[other, lanes], far_ref[:half, lanes]
-        values_same = ones_outside(v_ref[same, lanes])
-        values_other = ones_outside(v_ref[other, lanes])
-        values_far = ones_outside(far_ref[half:, lanes])
+        values = [
+            jnp.where(mask, ref.astype(f32), 1.0).astype(bf16)
+            for ref in (v_ref[:, lanes], far_ref[half:, lanes])
+        ]
         for part in range(rows // chunk):
             at = slice(part * chunk, (part + 1) * chunk)
-            in_pair = same.start <= at.start < same.stop
-            queries = jnp.where(mask, q_ref[at, lanes].astype(f32), 0.0).astype(bf16)
-            scores = [dot_nt(queries, keys_same), dot_nt(queries, keys_other)]
-            values = [values_same, values_other]
-            if in_pair:
-                scores.append(dot_nt(queries, keys_far))
-                values.append(values_far)
-            peaks = [jnp.max(s, axis=1, keepdims=True) for s in scores]
-            peak = functools.reduce(jnp.maximum, peaks) * SCALE
-            total = 0.0
-            for index, (s, v) in enumerate(zip(scores, values)):
-                shift = peak - 1.0 if in_pair and index == 0 else peak
-                total = total + dot(jnp.exp2(s * SCALE - shift).astype(bf16), v)
-            mass = total[:, outside : outside + 1]
-            out_ref[at, lanes] = jnp.where(mask, total * (1.0 / mass), out_ref[at, lanes])
-            lse_ref[at, lanes] = jnp.where(mask, peak + jnp.log2(mass), lse_ref[at, lanes])
-
-
-def attend_near(queries, key_rows, value_rows, far):
+            in_pair = at.start // half == h % 2
+            scores = score(h, at, in_pair)
+            if waiting is not None:
+                settle(*waiting)
+            waiting = (h, at, in_pair, scores, values)
+    settle(*waiting)
+
+
+def attend_near(side, queries, key_rows, value_rows, far):
     rows, width = queries.shape
-    spec = pl.BlockSpec((rows, 8 * HD), lambda i: (0, i))
+    spec = pl.BlockSpec((rows, 8 * HD), lambda i: (0, side))
     return pl.pallas_call(
         near_kernel,
-        grid=(width // (8 * HD),),
-        out_shape=[jax.ShapeDtypeStruct((rows, width), f32)] * 2,
+        grid=(1,),
+        out_shape=[jax.ShapeDtypeStruct((rows, 8 * HD), f32)] * 2,
         in_specs=[spec] * 4,
-        out_specs=[spec] * 2,
+        out_specs=[pl.BlockSpec((rows, 8 * HD), lambda i: (0, 0))] * 2,
+        scratch_shapes=[pltpu.VMEM((8 * HD, rows), bf16), pltpu.VMEM((8 * HD, rows // 2), bf16)],
         compiler_params=PARAMS,
         cost_estimate=pl.CostEstimate(
-            flops=12 * 10**9, bytes_accessed=10 * 1024 * 1024, transcendentals=12 * 10**6
+            flops=6 * 10**9, bytes_accessed=5 * 1024 * 1024, transcendentals=6 * 10**6
         ),
         name="near_attention",
     )(queries, key_rows, value_rows, far)
 
 
-def wide_kernel(repeat, part_ref, recv_ref, out_ref, keys, values):
+def wide_kernel(repeat, part_ref, recv_ref, out_ref, keys, values, turned):
     count, packed, _ = recv_ref.shape
     each = packed * 8 // 9
     tail_rows = each // 8
@@ -261,22 +287,40 @@
             picked = jnp.where(lane >= 96, wide[:each], jnp.where(lane < 16, tail, 1.0))
             values[at, :] = picked.astype(bf16)
 
-    queries = pltpu.roll(recv_ref[step * repeat + part_ref[0]].astype(f32)[:each], HD, axis=1)
-    queries = jnp.where((lane >= HD) & (lane < 2 * HD), queries, 0.0).astype(bf16)
-    scores = dot_nt(queries, keys[...])
-    peak = jnp.max(scores, axis=1, keepdims=True) * SCALE
-    total = dot(jnp.exp2(scores * SCALE - peak).astype(bf16), values[...])
-    total = pltpu.roll(total, 32, axis=1)
-    mass = total[:, HD : HD + 1]
-    lse = peak + jnp.log2(mass)
-    high, middle, low = [piece.astype(f32) for piece in split3(lse)]
-    out = jnp.where(
-        lane < HD,
-        total * (1.0 / mass),
-        jnp.where(lane == HD, high, jnp.where(lane == HD + 1, middle, low)),
-    )
-    upper = pltpu.roll(out[each // 2 :], 64, axis=1)
-    out_ref[0] = jnp.where(lane < 64, out[: each // 2], upper).astype(bf16)
+        for first in range(0, count * each, 256):
+            turned[:, first : first + 256] = keys[first : first + 256, :].T
+
+    def score(index, at):
+        block = recv_ref[(step * 2 + index) * repeat + part_ref[0]].astype(f32)
+        queries = pltpu.roll(block[at], HD, axis=1)
+        queries = jnp.where((lane >= HD) & (lane < 2 * HD), queries, 0.0).astype(bf16)
+        return dot(queries, turned[...])
+
+    def settle(scores):
+        peak = jnp.max(scores, axis=1, keepdims=True) * SCALE
+        total = dot(jnp.exp2(scores * SCALE - peak).astype(bf16), values[...])
+        total = pltpu.roll(total, 32, axis=1)
+        mass = total[:, HD : HD + 1]
+        lse = peak + jnp.log2(mass)
+        high, middle, low = [piece.astype(f32) for piece in split3(lse)]
+        return jnp.where(
+            lane < HD,
+            total * (1.0 / mass),
+            jnp.where(lane == HD, high, jnp.where(lane == HD + 1, middle, low)),
+        )
+
+    halves = [slice(0, each // 2), slice(each // 2, each)]
+    todo = [(index, at) for index in range(2) for at in halves]
+    done, waiting = [], None
+    for item in todo:
+        scores = score(*item)
+        if waiting is not None:
+            done.append(settle(waiting))
+        waiting = scores
+    done.append(settle(waiting))
+    for index in range(2):
+        upper = pltpu.roll(done[2 * index + 1], 64, axis=1)
+        out_ref[index] = jnp.where(lane < 64, done[2 * index], upper).astype(bf16)
 
 
 def attend_wide(repeat, part, received):
@@ -285,11 +329,12 @@
     steps = count // repeat
     return pl.pallas_call(
         functools.partial(wide_kernel, repeat),
-        grid=(steps,),
+        grid=(steps // 2,),
         out_shape=jax.ShapeDtypeStruct((steps, each // 2, LANES), bf16),
         in_specs=[SMEM, pl.BlockSpec(received.shape, lambda i: (0, 0, 0))],
-        out_specs=pl.BlockSpec((1, each // 2, LANES), lambda i: (i, 0, 0)),
-        scratch_shapes=[pltpu.VMEM((count * each, LANES), bf16)] * 2,
+        out_specs=pl.BlockSpec((2, each // 2, LANES), lambda i: (i, 0, 0)),
+        scratch_shapes=[pltpu.VMEM((count * each, LANES), bf16)] * 2
+        + [pltpu.VMEM((LANES, count * each), bf16)],
         compiler_params=PARAMS,
         cost_estimate=pl.CostEstimate(
             flops=10 * 10**9, bytes_accessed=2 * 1024 * 1024, transcendentals=10**7
@@ -298,13 +343,19 @@
     )(part, received)
 
 
-def finish_kernel(near_ref, lse_ref, wide_ref, out_w_ref, now_ref, out_ref, mixed):
-    rows, width = near_ref.shape
+def finish_kernel(
+    near_a_ref, lse_a_ref, near_b_ref, lse_b_ref, wide_ref, out_w_ref, now_ref, out_ref, mixed
+):
+    rows, width = now_ref.shape
+    side = width // 2
     each = rows // DILATION
-    mixed[...] = near_ref[...]
+    mixed[:, :side] = near_a_ref[...]
+    mixed[:, side:] = near_b_ref[...]
     for h in range(HEADS):
-        start, span, offset = window(h)
+        near_ref, lse_ref = ((near_a_ref, lse_a_ref), (near_b_ref, lse_b_ref))[h // 8]
+        start, span, offset = window(h % 8)
         lanes = slice(start, start + span)
+        placed = slice(start + h // 8 * side, start + h // 8 * side + span)
         mask = lane_mask(span, offset)
         first = BLOCK_OF[h % DILATION] * each
         at = slice(first, first + each)
@@ -318,25 +369,33 @@
         highest = jnp.maximum(near_lse, far_lse)
         near_weight, far_weight = jnp.exp2(near_lse - highest), jnp.exp2(far_lse - highest)
         merged = (near_weight * near_ref[at, lanes] + far_weight * far_out) / (near_weight + far_weight)
-        mixed[at, lanes] = jnp.where(mask, merged, mixed[at, lanes])
+        mixed[at, placed] = jnp.where(mask, merged, mixed[at, placed])
     attended = dot(permutation(rows, True), mixed[...].astype(bf16)).astype(bf16)
     out_ref[...] = (now_ref[...].astype(f32) + dot(attended, out_w_ref[...])).astype(bf16)
 
 
-def finish(near_out, near_lse, wide, out_full, slide_now):
+def finish(near_a, near_b, wide, gathered, slide_now):
     rows, width = slide_now.shape
+    half = pl.BlockSpec((rows, width // 2), lambda i: (0, 0))
+    whole = pl.BlockSpec((rows, width), lambda i: (0, 0))
     return pl.pallas_call(
         finish_kernel,
+        grid=(1,),
         out_shape=jax.ShapeDtypeStruct((rows, width), bf16),
-        in_specs=[VMEM] * 5,
-        out_specs=VMEM,
+        in_specs=[half] * 4
+        + [
+            pl.BlockSpec(wide.shape, lambda i: (0, 0, 0)),
+            pl.BlockSpec((width, width), lambda i: (0, 3)),
+            whole,
+        ],
+        out_specs=whole,
         scratch_shapes=[pltpu.VMEM((rows, width), f32)],
         compiler_params=PARAMS,
         cost_estimate=pl.CostEstimate(
             flops=4 * rows * width * width, bytes_accessed=9 * 1024 * 1024, transcendentals=0
         ),
         name="finish",
-    )(near_out, near_lse, wide, out_full, slide_now)
+    )(*near_a, *near_b, wide, gathered, slide_now)
 
 
 def body(tile_tokens, tile_counts, w_gate_up, w_down, w_tile_proj, slide_rows, w_qkv, w_out):
@@ -344,26 +403,31 @@
     repeat = size // HEADS
     me = lax.axis_index("slide")
     my_count = lax.dynamic_slice(tile_counts, (me,), (1,))
-    qkv_full = lax.all_gather(w_qkv, "slide", axis=0, tiled=True)
-    proj_full = lax.all_gather(w_tile_proj, "slide", axis=0, tiled=True)
-    out_full = lax.all_gather(w_out, "slide", axis=0, tiled=True)
+    piece = w_qkv.shape[0]
+    mine = jnp.concatenate([w_qkv, w_out, w_tile_proj[:piece], w_tile_proj[piece:]], axis=1)
+    gathered = lax.all_gather(mine, "slide", axis=0, tiled=True)
     embedded = encode_tiles(my_count, tile_tokens, w_gate_up, w_down)
     keep = jnp.arange(TMAX, dtype=jnp.int32)[:, None] < my_count
     tile_embeddings = jnp.where(keep, embedded[:TMAX], jnp.zeros((), bf16))
+    ordered = embedded.reshape(embedded.shape[0], size, 2, piece)
+    ordered = jnp.transpose(ordered, (2, 0, 1, 3)).reshape(2, embedded.shape[0], -1)
     slide_now, queries, key_rows, value_rows, far, send = project(
-        repeat, my_count, embedded, proj_full, slide_rows, qkv_full
+        repeat, my_count, ordered, slide_rows, gathered
     )
     far = lax.ppermute(far, "slide", [(source, source ^ 1) for source in range(size)])
     received = lax.all_to_all(send, "slide", 0, 0, tiled=True)
-    near_out, near_lse = attend_near(queries, key_rows, value_rows, far)
+    near_a = attend_near(0, queries, key_rows, value_rows, far)
+    received, near_a = lax.optimization_barrier((received, near_a))
     wide = attend_wide(repeat, (me % repeat).astype(jnp.int32)[None], received)
+    wide, queries = lax.optimization_barrier((wide, queries))
+    near_b = attend_near(1, queries, key_rows, value_rows, far)
     wide = jnp.repeat(wide, repeat, axis=0) if repeat > 1 else wide
     wide = lax.all_to_all(wide, "slide", 0, 0, tiled=True)
     if repeat > 1:
         wide = lax.dynamic_index_in_dim(
             wide.reshape(HEADS, repeat, *wide.shape[1:]), me % repeat, 1, keepdims=False
         )
-    return finish(near_out, near_lse, wide, out_full, slide_now), tile_embeddings
+    return finish(near_a, near_b, wide, gathered, slide_now), tile_embeddings
 
 
 def solution(mesh):

time: 228 us -> 173 us (0.76)
  waiting for transfers between devices: 99.4 us -> 59.4 us
  Pallas kernels: 96.5 us -> 78.7 us
    all_gather x3 -> x1, waiting for transfers between devices: 79.6 us -> 53.5 us  [body(): gathered = lax.all_gather(mine, 'slide', axis=0, tiled=True)]
    pallas_call x4 -> x5, Pallas kernels: 82.3 us -> 64.4 us  [the longest x2 25.2 us: attend_near(): pl.pallas_call(near_kernel, grid=(1,), out_shape=[jax.ShapeDtypeStruct((r...]
    all_to_all x1, waiting for transfers between devices: 17.8 us -> 5.8 us  [body(): received = lax.all_to_all(send, 'slide', 0, 0, tiled=True)]
  transfers between devices with their start and end apart: 6 -> 4, of which waited for: 3 -> 2; matrix products, arithmetic and copies ran while one was open for 1% -> 3% of each run, Pallas kernels for 34% -> 23%
where the time goes in v1:
time: 173 us; the launch traced here: 172 us
  Pallas kernels  78.7 us (45%)
  waiting for transfers between devices  59.4 us (34%)
  between operations  14.1 us (8%)
  starting transfers between devices  10.3 us (6%)
  local copies, waits for them, and re-layouts  6 us (3%)
  other arithmetic  3.83 us (2%)
    all_gather x1, waiting for transfers between devices, body(): gathered = lax.all_gather(mine, 'slide', axis=0, tiled=True)  53.5 us
    pallas_call x2, Pallas kernels, attend_near(): pl.pallas_call(near_kernel, grid=(1,), out_shape=[jax.ShapeDtypeStruct((r...  25.2 us
    pallas_call x1, Pallas kernels, attend_wide(): pl.pallas_call(functools.partial(wide_kernel, repeat), grid=(steps // 2,)...  19.8 us
    pallas_call x1, Pallas kernels, encode_tiles(): pl.pallas_call(tile_kernel, grid=(steps,), out_shape=jax.ShapeDtypeStruct...  14.3 us
    pallas_call x1, Pallas kernels, project(): pl.pallas_call(functools.partial(project_kernel, repeat), grid=(1,), out_...  12.1 us
    pallas_call x1, Pallas kernels, finish(): pl.pallas_call(finish_kernel, grid=(1,), out_shape=jax.ShapeDtypeStruct((...  7.34 us
    all_to_all x1, starting transfers between devices, body(): wide = lax.all_to_all(wide, 'slide', 0, 0, tiled=True)  6.19 us
    all_to_all x1, waiting for transfers between devices, body(): received = lax.all_to_all(send, 'slide', 0, 0, tiled=True)  5.8 us
  transfers between devices with their start and end apart: 4, of which 2 were waited for; matrix products, arithmetic and copies ran while one was open for 3% of the time, Pallas kernels for 23%

profile of v1, /device:TPU:0, one launch (start us, length us, event | category | flops | bytes accessed | tf_op | source)
XLA Modules:
  0.0 172.3 jit_solution(8032503848473710745)
XLA Ops:
  7.2 0.0 copy-start.3
  7.2 0.0 all-gather.2.cloned.1.call-start
  7.2 0.9 fusion
  8.2 1.8 %pad_maximum_fusion = bf16[48,4608]{1,0:T(8,128)(2,1)} fusion(bf16[48,768]{1,0:T(8,128)(2,1)S(1)} %get-tuple-element.33, bf16[48,768]{1,0:T(8,128)(2,1)S(1)} %get-tuple-element.32, bf16[48,768]{1,0:T(8,128)(2,1)} %param.15, bf16[48,2304]{1,0:T(8,128)(2,1)} %param.14), kind=kLoop, calls=%fused_computation | loop fusion | flops 1769472 | bytes 884736 | tf_op jit(solution)/shard_map/concatenate | solution.py:407
  9.9 0.0 all-gather.2.cloned.1.call-update
  9.9 0.0 copy-done.3
  10.0 0.6 dynamic_slice.3.count_ref
  10.5 14.3 %tile_block.1 = bf16[16,1536]{1,0:T(8,128)(2,1)} custom-call(s32[1]{0:T(128)} %dynamic_slice.3.count_ref, bf16[768,1536]{1,0:T(8,128)(2,1)} %tokens_ref.1, bf16[1536,4096]{1,0:T(8,128)(2,1)} %up_ref.1, bf16[1536,4096]{1,0:T(8,128)(2,1)} %up_ref.1, bf16[2048,1536]{1,0:T(8,128)(2,1)} %down_ref.1), custom_call_target="tpu_custom_call" | custom-call | flops 9663676416 | bytes 23068672 | tf_op jit(solution)/shard_map/tile_block/pallas_call | solution.py:111
  24.9 1.0 reshape.18
  25.9 0.8 reshape.19.emb_ref
  26.7 53.5 %all-gather.2.cloned.1.call-done.proj_ref.qkv_ref.out_w_ref = bf16[768,4608]{1,0:T(8,128)(2,1)} async-done(((bf16[48,4608]{1,0:T(8,128)(2,1)}), bf16[768,4608]{1,0:T(8,128)(2,1)}) %all-gather.2.cloned.1.call-update) | async-done | bytes 7077904 | tf_op jit(solution)/shard_map/all_gather | solution.py:408
  80.2 12.1 %project.1 = (bf16[768,768]{1,0:T(8,128)(2,1)}, bf16[768,768]{1,0:T(8,128)(2,1)}, bf16[768,768]{1,0:T(8,128)(2,1)}, bf16[768,768]{1,0:T(8,128)(2,1)}, bf16[768,7...) custom-call(s32[1]{0:T(128)} %dynamic_slice.3.count_ref, bf16[2,16,768]{2,1,0:T(8,128)(2,1)} %reshape.19.emb_ref, ...), custom_call_target="tpu_custom_call" | custom-call | flops 3623878656 | bytes 16777216 | tf_op jit(solution)/shard_map/project/pallas_call | solution.py:174
  92.3 0.3 collective-permute-start
  92.5 3.8 %all-to-all-start = ((bf16[16,216,128]{2,1,0:T(8,128)(2,1)}), bf16[16,216,128]{2,1,0:T(8,128)(2,1)S(1)}, u32[]{:S(2)}, u32[]{:S(2)}) async-start(bf16[16,216,128]{2,1,0:T(8,128)(2,1)} %get-tuple-element.17), calls=%async_computation | async-start | bytes 1769472 | tf_op jit(solution)/shard_map/all_to_all | solution.py:418
  96.4 0.7 iota_compare_fusion
  97.0 0.0 collective-permute-done.far_ref
  97.0 0.0 copy-start.2
  97.0 1.0 copy-done.2
  98.0 12.6 %near_attention.2 = (f32[768,384]{1,0:T(8,128)}, f32[768,384]{1,0:T(8,128)}) custom-call(bf16[768,768]{1,0:T(8,128)(2,1)} %get-tuple-element.27.q_ref, bf16[768,768]{1,0:T(8,128)(2,1)} %get-tuple-element.19.k_ref, bf16[768,768]{1,0:T(8,128)(2,1)} %get-tuple-element.20.v_ref, bf16[768,768]{1,0:T(8,128)(2,1)} %copy-done.2), custom_call_target="tpu_custom_call" | custom-call | flops 6000000000 | bytes 5242880 | tf_op jit(solution)/shard_map/near_attention/pallas_call | solution.py:254
  110.6 5.8 %all-to-all-done.recv_ref = bf16[16,216,128]{2,1,0:T(8,128)(2,1)S(1)} async-done(((bf16[16,216,128]{2,1,0:T(8,128)(2,1)}), bf16[16,216,128]{2,1,0:T(8,128)(2,1)S(1)}, u32[]{:S(2)}, u32[]{:S(2)}) %all-to-all-start) | async-done | bytes 884768 | tf_op jit(solution)/shard_map/all_to_all | solution.py:418
  116.4 0.0 copy-start.1
  116.4 0.9 copy-done.1
  117.4 19.8 %wide_attention.1 = bf16[16,96,128]{2,1,0:T(8,128)(2,1)} custom-call(s32[1]{0:T(128)} %constant.21.clone.1.part_ref, bf16[16,216,128]{2,1,0:T(8,128)(2,1)} %copy-done.1), custom_call_target="tpu_custom_call" | custom-call | flops 10000000000 | bytes 2097152 | tf_op jit(solution)/shard_map/wide_attention/pallas_call | solution.py:330
  137.2 6.2 %all-to-all-start.1 = ((bf16[16,96,128]{2,1,0:T(8,128)(2,1)}), bf16[16,96,128]{2,1,0:T(8,128)(2,1)S(1)}, u32[]{:S(2)}, u32[]{:S(2)}) async-start(bf16[16,96,128]{2,1,0:T(8,128)(2,1)} %wide_attention.1), calls=%async_computation.1 | async-start | bytes 786432 | tf_op jit(solution)/shard_map/all_to_all | solution.py:425
  143.4 1.4 slice_select_fusion
  144.8 12.6 %near_attention.3 = (f32[768,384]{1,0:T(8,128)}, f32[768,384]{1,0:T(8,128)}) custom-call(bf16[768,768]{1,0:T(8,128)(2,1)} %get-tuple-element.27.q_ref, bf16[768,768]{1,0:T(8,128)(2,1)} %get-tuple-element.19.k_ref, bf16[768,768]{1,0:T(8,128)(2,1)} %get-tuple-element.20.v_ref, bf16[768,768]{1,0:T(8,128)(2,1)} %copy-done.2), custom_call_target="tpu_custom_call" | custom-call | flops 6000000000 | bytes 5242880 | tf_op jit(solution)/shard_map/near_attention/pallas_call | solution.py:254
  157.4 0.0 all-to-all-done.1.wide_ref
  157.4 0.0 copy-start
  157.4 0.8 copy-done
  158.1 7.3 %finish.1 = bf16[768,768]{1,0:T(8,128)(2,1)} custom-call(f32[768,384]{1,0:T(8,128)} %get-tuple-element.24.near_a_ref, f32[768,384]{1,0:T(8,128)} %get-tuple-element.25.lse_a_ref, f32[768,384]{1,0:T(8,128)} %get-tuple-element.28.near_b_ref, f32[768,384]{1,0:T(8,128)} %get-tuple-element.29.lse_b_ref, bf16[16,96,128]{2,1,0:T(8,128)(2,1)} %copy-done, ...), custom_call_target="tpu_custom_call" | custom-call | flops 1811939328 | bytes 9437184 | tf_op jit(solution)/shard_map/finish/pallas_call | solution.py:381
  (1 shorter events, 0.0 us)
Async XLA Ops:
  7.2 2.8 %copy-start.3 = (s32[16]{0:T(128)S(1)}, s32[16]{0:T(128)}, u32[]{:S(2)}) copy-start(s32[16]{0:T(128)} %param.9) | copy-start | bytes 196
  7.2 73.0 %all-gather.2.cloned.1.call-start = ((), (), s32[]{:S(2)}) async-start(), calls=%async_computation.2 | async-start | bytes 7520256 | tf_op jit(solution)/shard_map/all_gather | solution.py:408
  92.3 4.7 %collective-permute-start = (bf16[768,768]{1,0:T(8,128)(2,1)}, bf16[768,768]{1,0:T(8,128)(2,1)S(1)}, u32[]{:S(2)}, u32[]{:S(2)}) collective-permute-start(bf16[768,768]{1,0:T(8,128)(2,1)} %get-tuple-element.21), channel_id=1, source_target_pairs={{0,1},{1,0},{2,3},{3,2},{4,5},{5,4},{6,7},{7,6},{8,9},{9,8},{10,11... | collective-permute-start | bytes 3538952 | tf_op jit(solution)/shard_map/ppermute | solution.py:417
  92.5 23.9 %all-to-all-start = ((bf16[16,216,128]{2,1,0:T(8,128)(2,1)}), bf16[16,216,128]{2,1,0:T(8,128)(2,1)S(1)}, u32[]{:S(2)}, u32[]{:S(2)}) async-start(bf16[16,216,128]{2,1,0:T(8,128)(2,1)} %get-tuple-element.17), calls=%async_computation | async-start | bytes 1769472 | tf_op jit(solution)/shard_map/all_to_all | solution.py:418
  97.0 1.0 copy-start.2
  116.4 0.9 copy-start.1
  137.2 20.2 %all-to-all-start.1 = ((bf16[16,96,128]{2,1,0:T(8,128)(2,1)}), bf16[16,96,128]{2,1,0:T(8,128)(2,1)S(1)}, u32[]{:S(2)}, u32[]{:S(2)}) async-start(bf16[16,96,128]{2,1,0:T(8,128)(2,1)} %wide_attention.1), calls=%async_computation.1 | async-start | bytes 786432 | tf_op jit(solution)/shard_map/all_to_all | solution.py:425
  157.4 0.8 copy-start
Sparse Core Ops, SparseCore 0:
  10.9 69.3 all-gather.1

commit v2 on v1

--- a/solution.py
+++ b/solution.py
@@ -130,12 +130,11 @@
 
 
 def project_kernel(
-    repeat, count_ref, emb_ref, proj_ref, rows_ref, qkv_ref, now_ref, q_ref, k_ref, v_ref, far_ref, send_ref
+    repeat, count_ref, fresh_ref, rows_ref, qkv_ref, now_ref, q_ref, k_ref, v_ref, far_ref, send_ref
 ):
     rows, width = rows_ref.shape
     each, half = rows // DILATION, rows // 2
-    fresh = dot(emb_ref[0], proj_ref[:, :width]) + dot(emb_ref[1], proj_ref[:, width:])
-    fresh = fresh.astype(bf16).astype(f32)
+    fresh = fresh_ref[...].astype(f32)
     keep = lax.broadcasted_iota(jnp.int32, (16, 1), 0) < count_ref[0]
     now_ref[...] = rows_ref[...]
     now_ref[0:16, :] = jnp.where(keep, fresh, rows_ref[0:16, :].astype(f32)).astype(bf16)
@@ -166,7 +165,7 @@
             send_ref[h * repeat + again] = whole
 
 
-def project(repeat, my_count, embedded, slide_rows, gathered):
+def project(repeat, my_count, fresh, slide_rows, qkv_full):
     rows, width = slide_rows.shape
     each = rows // DILATION
     square = jax.ShapeDtypeStruct((rows, width), bf16)
@@ -177,8 +176,7 @@
         out_shape=[square] * 5 + [jax.ShapeDtypeStruct(packed, bf16)],
         in_specs=[
             SMEM,
-            pl.BlockSpec(embedded.shape, lambda i: (0, 0, 0)),
-            pl.BlockSpec((width, 2 * width), lambda i: (0, 2)),
+            pl.BlockSpec(fresh.shape, lambda i: (0, 0)),
             pl.BlockSpec((rows, width), lambda i: (0, 0)),
             pl.BlockSpec((width, 3 * width), lambda i: (0, 0)),
         ],
@@ -189,7 +187,7 @@
             flops=2 * rows * width * 4 * width, bytes_accessed=16 * 1024 * 1024, transcendentals=0
         ),
         name="project",
-    )(my_count, embedded, gathered, slide_rows, gathered)
+    )(my_count, fresh, slide_rows, qkv_full)
 
 
 def near_kernel(q_ref, k_ref, v_ref, far_ref, out_ref, lse_ref, turned, turned_far):
@@ -374,7 +372,7 @@
     out_ref[...] = (now_ref[...].astype(f32) + dot(attended, out_w_ref[...])).astype(bf16)
 
 
-def finish(near_a, near_b, wide, gathered, slide_now):
+def finish(near_a, near_b, wide, out_full, slide_now):
     rows, width = slide_now.shape
     half = pl.BlockSpec((rows, width // 2), lambda i: (0, 0))
     whole = pl.BlockSpec((rows, width), lambda i: (0, 0))
@@ -385,7 +383,7 @@
         in_specs=[half] * 4
         + [
             pl.BlockSpec(wide.shape, lambda i: (0, 0, 0)),
-            pl.BlockSpec((width, width), lambda i: (0, 3)),
+            pl.BlockSpec((width, width), lambda i: (0, 0)),
             whole,
         ],
         out_specs=whole,
@@ -395,7 +393,7 @@
             flops=4 * rows * width * width, bytes_accessed=9 * 1024 * 1024, transcendentals=0
         ),
         name="finish",
-    )(*near_a, *near_b, wide, gathered, slide_now)
+    )(*near_a, *near_b, wide, out_full, slide_now)
 
 
 def body(tile_tokens, tile_counts, w_gate_up, w_down, w_tile_proj, slide_rows, w_qkv, w_out):
@@ -403,16 +401,22 @@
     repeat = size // HEADS
     me = lax.axis_index("slide")
     my_count = lax.dynamic_slice(tile_counts, (me,), (1,))
-    piece = w_qkv.shape[0]
-    mine = jnp.concatenate([w_qkv, w_out, w_tile_proj[:piece], w_tile_proj[piece:]], axis=1)
-    gathered = lax.all_gather(mine, "slide", axis=0, tiled=True)
+    qkv_full = lax.all_gather(w_qkv, "slide", axis=0, tiled=True)
+    w_out, qkv_full = lax.optimization_barrier((w_out, qkv_full))
+    out_full = lax.all_gather(w_out, "slide", axis=0, tiled=True)
     embedded = encode_tiles(my_count, tile_tokens, w_gate_up, w_down)
     keep = jnp.arange(TMAX, dtype=jnp.int32)[:, None] < my_count
     tile_embeddings = jnp.where(keep, embedded[:TMAX], jnp.zeros((), bf16))
-    ordered = embedded.reshape(embedded.shape[0], size, 2, piece)
-    ordered = jnp.transpose(ordered, (2, 0, 1, 3)).reshape(2, embedded.shape[0], -1)
+    piece, slide_width = w_tile_proj.shape
+    shares = jnp.transpose(embedded.reshape(-1, size, piece), (1, 0, 2))
+    shares = lax.all_to_all(shares, "slide", 0, 0, tiled=True)
+    terms = dot(shares.reshape(-1, piece), w_tile_proj).reshape(size, -1, slide_width)
+    terms = terms[:, :TMAX].reshape(size, -1, LANES)
+    terms = lax.all_to_all(terms, "slide", 0, 0, tiled=True)
+    fresh = jnp.sum(terms, axis=0).reshape(TMAX, slide_width).astype(bf16)
+    fresh = jnp.pad(fresh, ((0, 16 - TMAX), (0, 0)))
     slide_now, queries, key_rows, value_rows, far, send = project(
-        repeat, my_count, ordered, slide_rows, gathered
+        repeat, my_count, fresh, slide_rows, qkv_full
     )
     far = lax.ppermute(far, "slide", [(source, source ^ 1) for source in range(size)])
     received = lax.all_to_all(send, "slide", 0, 0, tiled=True)
@@ -427,7 +431,7 @@
         wide = lax.dynamic_index_in_dim(
             wide.reshape(HEADS, repeat, *wide.shape[1:]), me % repeat, 1, keepdims=False
         )
-    return finish(near_a, near_b, wide, gathered, slide_now), tile_embeddings
+    return finish(near_a, near_b, wide, out_full, slide_now), tile_embeddings
 
 
 def solution(mesh):

time: 173 us -> 158 us (0.913)
  waiting for transfers between devices: 59.4 us -> 7.32 us
  blocking collectives: 0 us -> 39.4 us
  Pallas kernels: 78.7 us -> 76.4 us
  other arithmetic: 3.83 us -> 2.09 us
    all_gather x1 -> x2, waiting for transfers between devices: 53.5 us -> 0.01 us  [the longest x1 0.01 us: body(): qkv_full = lax.all_gather(w_qkv, 'slide', axis=0, tiled=True)]
    all_to_all x0 -> x2, blocking collectives: none -> 39.4 us  [the longest x1 27.5 us: body(): shares = lax.all_to_all(shares, 'slide', 0, 0, tiled=True)]
    pallas_call x1, Pallas kernels: 12.1 us -> 10.1 us  [project(): pl.pallas_call(functools.partial(project_kernel, repeat), grid=(1,), out_...]
    concatenate x1 -> x0, other arithmetic: 1.77 us -> none  [body(): jnp.concatenate([w_qkv, w_out, w_tile_proj[:piece], w_tile_proj[piece:]],...]
  transfers between devices with their start and end apart: 4 -> 5, of which waited for: 2 -> 1; matrix products, arithmetic and copies ran while one was open for 3% -> 3% of each run, Pallas kernels for 23% -> 38%
where the time goes in v2:
time: 158 us; the launch traced here: 157 us
  Pallas kernels  76.4 us (48%)
  blocking collectives  39.4 us (25%)
  between operations  14.1 us (9%)
  starting transfers between devices  11.4 us (7%)
  waiting for transfers between devices  7.32 us (5%)
  local copies, waits for them, and re-layouts  5.68 us (4%)
  other arithmetic  2.09 us (1%)
    all_to_all x1, blocking collectives, body(): shares = lax.all_to_all(shares, 'slide', 0, 0, tiled=True)  27.5 us
    pallas_call x2, Pallas kernels, attend_near(): pl.pallas_call(near_kernel, grid=(1,), out_shape=[jax.ShapeDtypeStruct((r...  25.1 us
    pallas_call x1, Pallas kernels, attend_wide(): pl.pallas_call(functools.partial(wide_kernel, repeat), grid=(steps // 2,)...  19.8 us
    pallas_call x1, Pallas kernels, encode_tiles(): pl.pallas_call(tile_kernel, grid=(steps,), out_shape=jax.ShapeDtypeStruct...  14.1 us
    all_to_all x1, blocking collectives, body(): terms = lax.all_to_all(terms, 'slide', 0, 0, tiled=True)  11.9 us
    pallas_call x1, Pallas kernels, project(): pl.pallas_call(functools.partial(project_kernel, repeat), grid=(1,), out_...  10.1 us
    all_to_all x1, starting transfers between devices, body(): wide = lax.all_to_all(wide, 'slide', 0, 0, tiled=True)  7.41 us
    pallas_call x1, Pallas kernels, finish(): pl.pallas_call(finish_kernel, grid=(1,), out_shape=jax.ShapeDtypeStruct((...  7.34 us
  transfers between devices with their start and end apart: 5, of which 1 were waited for; matrix products, arithmetic and copies ran while one was open for 3% of the time, Pallas kernels for 38%

profile of v2, /device:TPU:0, one launch (start us, length us, event | category | flops | bytes accessed | tf_op | source)
XLA Modules:
  0.0 156.6 jit_solution(5282076923089590020)
XLA Ops:
  7.2 0.0 copy-start
  7.2 0.0 all-gather.3.cloned.1.call-start
  7.2 0.7 all-gather.3.cloned.1.call-update
  7.9 1.2 dynamic_slice.3.count_ref
  9.2 14.1 %tile_block.1 = bf16[16,1536]{1,0:T(8,128)(2,1)} custom-call(s32[1]{0:T(128)} %dynamic_slice.3.count_ref, bf16[768,1536]{1,0:T(8,128)(2,1)} %tokens_ref.1, bf16[1536,4096]{1,0:T(8,128)(2,1)} %up_ref.1, bf16[1536,4096]{1,0:T(8,128)(2,1)} %up_ref.1, bf16[2048,1536]{1,0:T(8,128)(2,1)} %down_ref.1), custom_call_target="tpu_custom_call" | custom-call | flops 9663676416 | bytes 23068672 | tf_op jit(solution)/shard_map/tile_block/pallas_call | solution.py:111
  23.3 0.9 reshape.24
  24.2 27.5 %all_to_all.20 = bf16[16,16,96]{2,1,0:T(8,128)(2,1)S(1)} all-to-all(bf16[16,16,96]{2,1,0:T(8,128)(2,1)S(1)} %bitcast.7), channel_id=1, replica_groups=mesh['groups'=2,'slide'=16] {'slide'}, dimensions={0} | all-to-all | bytes 98304 | tf_op jit(solution)/shard_map/all_to_all | solution.py:412
  51.7 0.0 copy-done
  51.7 0.2 fusion
  51.9 0.1 reshape.25
  52.0 11.9 %all_to_all.21 = f32[16,18,128]{2,1,0:T(8,128)S(1)} all-to-all(f32[16,18,128]{2,1,0:T(8,128)S(1)} %reshape.25), channel_id=1, replica_groups=mesh['groups'=2,'slide'=16] {'slide'}, dimensions={0} | all-to-all | bytes 294912 | tf_op jit(solution)/shard_map/all_to_all | solution.py:415
  63.9 0.6 pad.4.fresh_ref
  64.5 0.0 all-gather.3.cloned.1.call-done.qkv_ref
  64.5 10.1 %project.1 = (bf16[768,768]{1,0:T(8,128)(2,1)}, bf16[768,768]{1,0:T(8,128)(2,1)}, bf16[768,768]{1,0:T(8,128)(2,1)}, bf16[768,768]{1,0:T(8,128)(2,1)}, bf16[768,7...) custom-call(s32[1]{0:T(128)} %dynamic_slice.3.count_ref, bf16[16,768]{1,0:T(8,128)(2,1)} %pad.4.fresh_ref, ...), custom_call_target="tpu_custom_call" | custom-call | flops 3623878656 | bytes 16777216 | tf_op jit(solution)/shard_map/project/pallas_call | solution.py:173
  74.6 0.0 collective-permute-start
  74.6 3.8 %all-to-all-start.2 = ((bf16[16,216,128]{2,1,0:T(8,128)(2,1)}), bf16[16,216,128]{2,1,0:T(8,128)(2,1)S(1)}, u32[]{:S(2)}, u32[]{:S(2)}) async-start(bf16[16,216,128]{2,1,0:T(8,128)(2,1)} %get-tuple-element.20), calls=%async_computation.2 | async-start | bytes 1769472 | tf_op jit(solution)/shard_map/all_to_all | solution.py:422
  78.3 0.2 all-gather.5.cloned.1.call-start
  78.6 0.7 iota_compare_fusion
  79.2 0.0 all-gather.5.cloned.1.call-update
  79.2 0.0 collective-permute-done.far_ref
  79.2 0.0 copy-start.3
  79.3 1.0 copy-done.3
  80.3 12.5 %near_attention.2 = (f32[768,384]{1,0:T(8,128)}, f32[768,384]{1,0:T(8,128)}) custom-call(bf16[768,768]{1,0:T(8,128)(2,1)} %get-tuple-element.30.q_ref, bf16[768,768]{1,0:T(8,128)(2,1)} %get-tuple-element.22.k_ref, bf16[768,768]{1,0:T(8,128)(2,1)} %get-tuple-element.23.v_ref, bf16[768,768]{1,0:T(8,128)(2,1)} %copy-done.3), custom_call_target="tpu_custom_call" | custom-call | flops 6000000000 | bytes 5242880 | tf_op jit(solution)/shard_map/near_attention/pallas_call | solution.py:252
  92.8 6.6 %all-to-all-done.2.recv_ref = bf16[16,216,128]{2,1,0:T(8,128)(2,1)S(1)} async-done(((bf16[16,216,128]{2,1,0:T(8,128)(2,1)}), bf16[16,216,128]{2,1,0:T(8,128)(2,1)S(1)}, u32[]{:S(2)}, u32[]{:S(2)}) %all-to-all-start.2) | async-done | bytes 884768 | tf_op jit(solution)/shard_map/all_to_all | solution.py:422
  99.4 0.0 copy-start.2
  99.4 1.0 copy-done.2
  100.4 19.8 %wide_attention.1 = bf16[16,96,128]{2,1,0:T(8,128)(2,1)} custom-call(s32[1]{0:T(128)} %constant.25.clone.1.part_ref, bf16[16,216,128]{2,1,0:T(8,128)(2,1)} %copy-done.2), custom_call_target="tpu_custom_call" | custom-call | flops 10000000000 | bytes 2097152 | tf_op jit(solution)/shard_map/wide_attention/pallas_call | solution.py:328
  120.2 7.4 %all-to-all-start.3 = ((bf16[16,96,128]{2,1,0:T(8,128)(2,1)}), bf16[16,96,128]{2,1,0:T(8,128)(2,1)S(1)}, u32[]{:S(2)}, u32[]{:S(2)}) async-start(bf16[16,96,128]{2,1,0:T(8,128)(2,1)} %wide_attention.1), calls=%async_computation.3 | async-start | bytes 786432 | tf_op jit(solution)/shard_map/all_to_all | solution.py:429
  127.6 1.4 slice_select_fusion
  129.0 12.6 %near_attention.3 = (f32[768,384]{1,0:T(8,128)}, f32[768,384]{1,0:T(8,128)}) custom-call(bf16[768,768]{1,0:T(8,128)(2,1)} %get-tuple-element.30.q_ref, bf16[768,768]{1,0:T(8,128)(2,1)} %get-tuple-element.22.k_ref, bf16[768,768]{1,0:T(8,128)(2,1)} %get-tuple-element.23.v_ref, bf16[768,768]{1,0:T(8,128)(2,1)} %copy-done.3), custom_call_target="tpu_custom_call" | custom-call | flops 6000000000 | bytes 5242880 | tf_op jit(solution)/shard_map/near_attention/pallas_call | solution.py:252
  141.6 0.0 all-gather.5.cloned.1.call-done.out_w_ref
  141.6 0.0 all-to-all-done.3.wide_ref
  141.6 0.0 copy-start.1
  141.6 0.7 copy-done.1
  142.4 7.3 %finish.1 = bf16[768,768]{1,0:T(8,128)(2,1)} custom-call(f32[768,384]{1,0:T(8,128)} %get-tuple-element.27.near_a_ref, f32[768,384]{1,0:T(8,128)} %get-tuple-element.28.lse_a_ref, f32[768,384]{1,0:T(8,128)} %get-tuple-element.31.near_b_ref, f32[768,384]{1,0:T(8,128)} %get-tuple-element.32.lse_b_ref, bf16[16,96,128]{2,1,0:T(8,128)(2,1)} %copy-done.1, ...), custom_call_target="tpu_custom_call" | custom-call | flops 1811939328 | bytes 9437184 | tf_op jit(solution)/shard_map/finish/pallas_call | solution.py:379
  (3 shorter events, 0.1 us)
Async XLA Ops:
  7.2 44.6 %copy-start = (bf16[96,768]{1,0:T(8,128)(2,1)S(1)}, bf16[96,768]{1,0:T(8,128)(2,1)}, u32[]{:S(2)}) copy-start(bf16[96,768]{1,0:T(8,128)(2,1)} %param.12) | copy-start | bytes 442372
  7.2 57.3 %all-gather.3.cloned.1.call-start = ((), (), s32[]{:S(2)}) async-start(), calls=%async_computation.4 | async-start | bytes 3760128 | tf_op jit(solution)/shard_map/all_gather | solution.py:404
  74.6 4.7 %collective-permute-start = (bf16[768,768]{1,0:T(8,128)(2,1)}, bf16[768,768]{1,0:T(8,128)(2,1)S(1)}, u32[]{:S(2)}, u32[]{:S(2)}) collective-permute-start(bf16[768,768]{1,0:T(8,128)(2,1)} %get-tuple-element.24), channel_id=1, source_target_pairs={{0,1},{1,0},{2,3},{3,2},{4,5},{5,4},{6,7},{7,6},{8,9},{9,8},{10,11... | collective-permute-start | bytes 3538952 | tf_op jit(solution)/shard_map/ppermute | solution.py:421
  74.6 24.8 %all-to-all-start.2 = ((bf16[16,216,128]{2,1,0:T(8,128)(2,1)}), bf16[16,216,128]{2,1,0:T(8,128)(2,1)S(1)}, u32[]{:S(2)}, u32[]{:S(2)}) async-start(bf16[16,216,128]{2,1,0:T(8,128)(2,1)} %get-tuple-element.20), calls=%async_computation.2 | async-start | bytes 1769472 | tf_op jit(solution)/shard_map/all_to_all | solution.py:422
  78.3 63.3 %all-gather.5.cloned.1.call-start = ((), (), s32[]{:S(2)}) async-start(), calls=%async_computation.5 | async-start | bytes 1253376 | tf_op jit(solution)/shard_map/all_gather | solution.py:406
  79.2 1.0 copy-start.3
  99.4 1.0 copy-start.2
  120.2 21.4 %all-to-all-start.3 = ((bf16[16,96,128]{2,1,0:T(8,128)(2,1)}), bf16[16,96,128]{2,1,0:T(8,128)(2,1)S(1)}, u32[]{:S(2)}, u32[]{:S(2)}) async-start(bf16[16,96,128]{2,1,0:T(8,128)(2,1)} %wide_attention.1), calls=%async_computation.3 | async-start | bytes 786432 | tf_op jit(solution)/shard_map/all_to_all | solution.py:429
  141.6 0.7 copy-start.1
Sparse Core Ops, SparseCore 0:
  10.3 52.0 all-gather.2
  81.4 41.3 all-gather.4
